TPU v7x, 32 devices: a whole 2x2x4 slice. The times are simulated.
32 devices in a mesh: rows: 8 (over z, y), feat: 4 (over x, core).
Axes of the slice: x: 2, y: 2, z: 4, core: 2. Of those that a mesh axis runs over, the one named last changes fastest.
Arguments:
- node_feats: float32 [256, 8192], P('feat', 'rows'), may hold values from -6 to 6
- theta: float32 [256, 256], P(None, 'feat'), may hold values from -0.375 to 0.375
- cotangent: float32 [256, 8192], P('feat', 'rows'), may hold values from -6 to 6
- remote_mol: int32 [64, 2], P('rows'), may hold values from 0 to 15
- remote_rxn: int32 [64, 2], P('rows'), may hold values from 0 to 15
- remote_count: int32 [64], P('rows'), may hold values from 0 to 2, as said below
- remote_tiles: int32 [64, 2, 4096], P('rows'), may hold values 0 or 1
- local_mol: int32 [256], P('rows'), may hold values from 0 to 15
- local_rxn: int32 [256], P('rows'), may hold values from 0 to 15
- local_tiles: int32 [256, 4096], P('rows'), may hold values 0 or 1
Outputs:
- out_feats: float32 [256, 8192], P('feat', 'rows')
- theta_grad: float32 [256, 256], P(None, 'feat')
Inputs may be any that keep to these rules, and one draw needn't show every extreme that they name: `remote_count`: for each source index, the live slots to each destination; one destination is filled to 2 from every source.
All inputs are finite; a program needn't handle non-finite values. No bound on the sum of `remote_tiles` or of `local_tiles` on one device may be relied on, other than what follows from the above.
Results may differ from a plain program's by a relative error of at most 0.0001.
Values sent between devices are 32-bit elements; how exact they have to be, the bound alone decides.
A program may use at most 128 MiB of HBM per device.

v0:
```python
import jax
import jax.numpy as jnp
from jax import lax
from jax.sharding import PartitionSpec as P

BLK = 64
MB_DEV = 16
RB_DEV = 16
CAP = 2


def to_blocks(values):
    width = values.shape[0]
    return values.reshape(width, MB_DEV, BLK).transpose(1, 0, 2)


def from_blocks(blocks):
    width = blocks.shape[1]
    return blocks.transpose(1, 0, 2).reshape(width, MB_DEV * BLK)


def widen(values):
    return lax.all_gather(values, "feat", axis=0, tiled=True)


def on_device(
    node_feats,
    theta,
    cotangent,
    remote_mol,
    remote_rxn,
    remote_count,
    remote_tiles,
    local_mol,
    local_rxn,
    local_tiles,
):
    highest = lax.Precision.HIGHEST
    nrows = lax.axis_size("rows")
    slots = nrows * CAP
    slot_live = (jnp.arange(CAP, dtype=jnp.int32)[None, :] < remote_count[:, None]).astype(
        jnp.float32
    )
    rtiles = (
        remote_tiles.astype(jnp.float32).reshape(nrows, CAP, BLK, BLK) * slot_live[:, :, None, None]
    ).reshape(slots, BLK, BLK)
    ltiles = local_tiles.astype(jnp.float32).reshape(-1, BLK, BLK)
    rmol = remote_mol.reshape(slots)
    sent_count = jnp.sum(rtiles, axis=1).astype(jnp.int32).reshape(nrows, CAP, BLK)
    idx_in, count_in = (
        lax.all_to_all(remote_rxn, "rows", split_axis=0, concat_axis=0, tiled=True),
        lax.all_to_all(sent_count, "rows", split_axis=0, concat_axis=0, tiled=True),
    )
    rxn_in = idx_in.reshape(slots)
    rxn_ids = jnp.arange(RB_DEV, dtype=jnp.int32)
    mol_ids = jnp.arange(MB_DEV, dtype=jnp.int32)
    recv_hot = (rxn_in[:, None] == rxn_ids[None, :]).astype(jnp.float32)
    local_rhot = (local_rxn[:, None] == rxn_ids[None, :]).astype(jnp.float32)
    remote_mhot = (rmol[:, None] == mol_ids[None, :]).astype(jnp.float32)
    local_mhot = (local_mol[:, None] == mol_ids[None, :]).astype(jnp.float32)
    edge_deg = 1.0 + jnp.einsum(
        "sr,sj->rj", recv_hot, count_in.reshape(slots, BLK).astype(jnp.float32), precision=highest
    )
    edge_deg = edge_deg + jnp.einsum(
        "sr,sj->rj", local_rhot, jnp.sum(ltiles, axis=1), precision=highest
    )
    vert_deg = 1.0 + jnp.einsum(
        "sm,si->mi", remote_mhot, jnp.sum(rtiles, axis=2), precision=highest
    )
    vert_deg = vert_deg + jnp.einsum(
        "sm,si->mi", local_mhot, jnp.sum(ltiles, axis=2), precision=highest
    )
    vscale = 1.0 / jnp.sqrt(vert_deg)

    def propagate(blocks):
        width = blocks.shape[1]
        scaled = blocks * vscale[:, None, :]
        rpart = jnp.einsum(
            "sci,sij->scj", jnp.take(scaled, rmol, axis=0), rtiles, precision=highest
        )
        recv = lax.all_to_all(
            rpart.reshape(nrows, CAP, width * BLK), "rows", split_axis=0, concat_axis=0, tiled=True
        ).reshape(slots, width, BLK)
        lpart = jnp.einsum(
            "sci,sij->scj", jnp.take(scaled, local_mol, axis=0), ltiles, precision=highest
        )
        acc = jnp.einsum("sr,scj->rcj", recv_hot, recv, precision=highest)
        acc = acc + jnp.einsum("sr,scj->rcj", local_rhot, lpart, precision=highest)
        edge = acc / edge_deg[:, None, :]
        outgoing = jnp.take(edge, rxn_in, axis=0).reshape(nrows, CAP, width * BLK)
        back = lax.all_to_all(outgoing, "rows", split_axis=0, concat_axis=0, tiled=True).reshape(
            slots, width, BLK
        )
        rmolp = jnp.einsum("sij,scj->sci", rtiles, back, precision=highest)
        lmolp = jnp.einsum(
            "sij,scj->sci", ltiles, jnp.take(edge, local_rxn, axis=0), precision=highest
        )
        accm = jnp.einsum("sm,sci->mci", remote_mhot, rmolp, precision=highest)
        accm = accm + jnp.einsum("sm,sci->mci", local_mhot, lmolp, precision=highest)
        return accm * vscale[:, None, :]

    gathered = widen(node_feats)
    hidden = jnp.einsum("fc,fm->cm", theta, gathered, precision=highest)
    mixed = from_blocks(propagate(to_blocks(hidden)))
    output = jnp.tanh(mixed)
    grad_mixed = cotangent * (1.0 - output * output)
    grad_hidden = from_blocks(propagate(to_blocks(grad_mixed)))
    partial_grad = jnp.einsum("fm,cm->fc", gathered, grad_hidden, precision=highest)
    theta_grad = lax.psum(partial_grad, "rows")
    return (output, theta_grad)


def solution(mesh):
    return jax.shard_map(
        on_device,
        mesh=mesh,
        in_specs=(
            P("feat", "rows"),
            P(None, "feat"),
            P("feat", "rows"),
            P("rows", None),
            P("rows", None),
            P("rows"),
            P("rows", None, None),
            P("rows"),
            P("rows"),
            P("rows", None),
        ),
        out_specs=(P("feat", "rows"), P(None, "feat")),
        check_vma=False,
    )
```

profile of v0, /device:TPU:0, one launch (start us, length us, event | category | flops | bytes accessed | tf_op | source)
XLA Modules:
  0.0 183.8 jit_solution(1202700141776858269)
XLA Ops:
  9.3 7.4 %all-to-all-start = ((s32[8,1,2]{2,1,0:T(1,128)}), s32[8,1,2]{2,1,0:T(1,128)S(1)}, u32[]{:S(2)}, u32[]{:S(2)}) async-start(s32[8,1,2]{2,1,0:T(1,128)} %copy.40), calls=%async_computation | async-start | bytes 8192 | tf_op jit(solution)/shard_map/all_to_all | solution.py:51
  23.1 5.2 %all-to-all-start.2 = ((s32[8,1,128]{2,1,0:T(1,128)}), s32[8,1,128]{2,1,0:T(1,128)S(1)}, u32[]{:S(2)}, u32[]{:S(2)}) async-start(s32[8,1,128]{2,1,0:T(1,128)} %reshape.213), calls=%async_computation.2 | async-start | bytes 8192 | tf_op jit(solution)/shard_map/all_to_all | solution.py:52
  29.6 5.1 %all-to-all-done.2 = s32[8,1,128]{2,1,0:T(1,128)S(1)} async-done(((s32[8,1,128]{2,1,0:T(1,128)}), s32[8,1,128]{2,1,0:T(1,128)S(1)}, u32[]{:S(2)}, u32[]{:S(2)}) %all-to-all-start.2) | async-done | bytes 4128 | tf_op jit(solution)/shard_map/all_to_all | solution.py:52
  36.2 2.0 %fusion.88 = f32[64,1024]{1,0:T(8,128)S(1)} fusion(f32[256,64]{0,1:T(8,128)S(1)} %copy-done, f32[256,1024]{1,0:T(8,128)} %all-gather.2.cloned.1.call-done), kind=kOutput, calls=%fused_computation.121 | convolution fusion | flops 201326592 | bytes 1376256 | tf_op jit(solution)/shard_map/fc,fm->cm/dot_general | solution.py:103
  40.9 3.4 %all-to-all-start.1 = ((f32[8,2,4096]{2,1,0:T(2,128)}), f32[8,2,4096]{2,1,0:T(2,128)S(1)}, u32[]{:S(2)}, u32[]{:S(2)}) async-start(f32[8,2,4096]{2,1,0:T(2,128)} %reshape.101), calls=%async_computation.1 | async-start | bytes 524288 | tf_op jit(solution)/shard_map/all_to_all | solution.py:81
  44.9 1.3 fusion.22
  47.2 5.2 %all-to-all-done.1 = f32[8,2,4096]{2,1,0:T(2,128)S(1)} async-done(((f32[8,2,4096]{2,1,0:T(2,128)}), f32[8,2,4096]{2,1,0:T(2,128)S(1)}, u32[]{:S(2)}, u32[]{:S(2)}) %all-to-all-start.1) | async-done | bytes 262176 | tf_op jit(solution)/shard_map/all_to_all | solution.py:81
  55.3 3.6 %all-to-all-start.3 = ((f32[8,2,4096]{2,1,0:T(2,128)}), f32[8,2,4096]{2,1,0:T(2,128)S(1)}, u32[]{:S(2)}, u32[]{:S(2)}) async-start(f32[8,2,4096]{2,1,0:T(2,128)} %reshape.103), calls=%async_computation.3 | async-start | bytes 524288 | tf_op jit(solution)/shard_map/all_to_all | solution.py:91
  59.5 1.9 %fusion.20 = f32[32,64,64]{2,1,0:T(8,128)S(1)} fusion(f32[32,64,64]{2,1,0:T(8,128)S(1)} %reshape.100, f32[32,64,64]{2,1,0:T(8,128)S(1)} %gather_fusion.3, pred[32]{0:T(512)(128)(4,1)S(1)} %compare_and_fusion), kind=kOutput, calls=%fused_computation.37 | convolution fusion | flops 100794368 | bytes 1572896 | tf_op jit(solution)/shard_map/sij,scj->sci/dot_general | solution.py:95
  62.5 4.4 %all-to-all-done.3 = f32[8,2,4096]{2,1,0:T(2,128)S(1)} async-done(((f32[8,2,4096]{2,1,0:T(2,128)}), f32[8,2,4096]{2,1,0:T(2,128)S(1)}, u32[]{:S(2)}, u32[]{:S(2)}) %all-to-all-start.3) | async-done | bytes 262176 | tf_op jit(solution)/shard_map/all_to_all | solution.py:91
  71.0 1.4 gather_fusion.4
  73.0 1.8 fusion.30
  75.8 3.4 %all-to-all-start.4 = ((f32[8,2,4096]{2,1,0:T(2,128)}), f32[8,2,4096]{2,1,0:T(2,128)S(1)}, u32[]{:S(2)}, u32[]{:S(2)}) async-start(f32[8,2,4096]{2,1,0:T(2,128)} %reshape.106), calls=%async_computation.4 | async-start | bytes 524288 | tf_op jit(solution)/shard_map/all_to_all | solution.py:81
  79.2 1.3 fusion.18
  80.4 1.1 fusion.10
  81.5 5.8 %all-to-all-done.4 = f32[8,2,4096]{2,1,0:T(2,128)S(1)} async-done(((f32[8,2,4096]{2,1,0:T(2,128)}), f32[8,2,4096]{2,1,0:T(2,128)S(1)}, u32[]{:S(2)}, u32[]{:S(2)}) %all-to-all-start.4) | async-done | bytes 262176 | tf_op jit(solution)/shard_map/all_to_all | solution.py:81
  88.6 1.4 gather_fusion.6
  90.6 1.1 broadcast_select_fusion
  92.7 3.4 %all-to-all-start.5 = ((f32[8,2,4096]{2,1,0:T(2,128)}), f32[8,2,4096]{2,1,0:T(2,128)S(1)}, u32[]{:S(2)}, u32[]{:S(2)}) async-start(f32[8,2,4096]{2,1,0:T(2,128)} %reshape.108), calls=%async_computation.5 | async-start | bytes 524288 | tf_op jit(solution)/shard_map/all_to_all | solution.py:91
  96.4 1.9 %fusion.16 = f32[32,64,64]{2,1,0:T(8,128)S(1)} fusion(f32[32,64,64]{2,1,0:T(8,128)S(1)} %reshape.100, f32[32,64,64]{2,1,0:T(8,128)S(1)} %gather_fusion.7, pred[32]{0:T(512)(128)(4,1)S(1)} %compare_and_fusion), kind=kOutput, calls=%fused_computation.33 | convolution fusion | flops 100794368 | bytes 1572896 | tf_op jit(solution)/shard_map/sij,scj->sci/dot_general | solution.py:95
  99.4 4.9 %all-to-all-done.5 = f32[8,2,4096]{2,1,0:T(2,128)S(1)} async-done(((f32[8,2,4096]{2,1,0:T(2,128)}), f32[8,2,4096]{2,1,0:T(2,128)S(1)}, u32[]{:S(2)}, u32[]{:S(2)}) %all-to-all-start.5) | async-done | bytes 262176 | tf_op jit(solution)/shard_map/all_to_all | solution.py:91
  106.9 1.7 convolution_bitcast_fusion
  108.6 66.9 %all-reduce.2.cloned.1.call-done = f32[256,64]{0,1:T(8,128)} async-done(((f32[256,64]{0,1:T(8,128)}), f32[256,64]{0,1:T(8,128)}) %all-reduce.2.cloned.1.call-update) | async-done | bytes 65552 | tf_op jit(solution)/shard_map/psum | solution.py:109
  175.5 1.5 copy.78
  (98 shorter events, 32.3 us)
Async XLA Ops:
  7.2 29.1 %copy-start = (f32[256,64]{0,1:T(8,128)S(1)}, f32[256,64]{0,1:T(8,128)}, u32[]{:S(2)}) copy-start(f32[256,64]{0,1:T(8,128)} %param.15) | copy-start | bytes 196612
  7.2 11.9 %copy-start.5 = (s32[8,2,4096]{2,1,0:T(2,128)S(1)}, s32[8,2,4096]{2,1,0:T(2,128)}, u32[]{:S(2)}) copy-start(s32[8,2,4096]{2,1,0:T(2,128)} %param.20) | copy-start | bytes 786436
  7.2 29.0 %all-gather.2.cloned.1.call-start = ((), (), s32[]{:S(2)}) async-start(), calls=%async_computation.6 | async-start | bytes 1310720 | tf_op jit(solution)/shard_map/all_gather | solution.py:23
  7.9 0.7 copy-start.8
  9.3 7.4 %copy-start.7 = (s32[32]{0:T(128)S(1)}, s32[32]{0:T(128)}, u32[]{:S(2)}) copy-start(s32[32]{0:T(128)} %param.21) | copy-start | bytes 388
  9.3 13.8 %all-to-all-start = ((s32[8,1,2]{2,1,0:T(1,128)}), s32[8,1,2]{2,1,0:T(1,128)S(1)}, u32[]{:S(2)}, u32[]{:S(2)}) async-start(s32[8,1,2]{2,1,0:T(1,128)} %copy.40), calls=%async_computation | async-start | bytes 8192 | tf_op jit(solution)/shard_map/all_to_all | solution.py:51
  16.7 0.7 copy-start.6
  17.4 0.7 copy-start.9
  18.2 0.7 copy-start.10
  19.1 1.1 copy-start.3
  23.1 11.6 %all-to-all-start.2 = ((s32[8,1,128]{2,1,0:T(1,128)}), s32[8,1,128]{2,1,0:T(1,128)S(1)}, u32[]{:S(2)}, u32[]{:S(2)}) async-start(s32[8,1,128]{2,1,0:T(1,128)} %reshape.213), calls=%async_computation.2 | async-start | bytes 8192 | tf_op jit(solution)/shard_map/all_to_all | solution.py:52
  40.9 11.6 %all-to-all-start.1 = ((f32[8,2,4096]{2,1,0:T(2,128)}), f32[8,2,4096]{2,1,0:T(2,128)S(1)}, u32[]{:S(2)}, u32[]{:S(2)}) async-start(f32[8,2,4096]{2,1,0:T(2,128)} %reshape.101), calls=%async_computation.1 | async-start | bytes 524288 | tf_op jit(solution)/shard_map/all_to_all | solution.py:81
  55.3 11.6 %all-to-all-start.3 = ((f32[8,2,4096]{2,1,0:T(2,128)}), f32[8,2,4096]{2,1,0:T(2,128)S(1)}, u32[]{:S(2)}, u32[]{:S(2)}) async-start(f32[8,2,4096]{2,1,0:T(2,128)} %reshape.103), calls=%async_computation.3 | async-start | bytes 524288 | tf_op jit(solution)/shard_map/all_to_all | solution.py:91
  69.0 1.0 copy-start.4
  69.9 0.7 copy-start.2
  75.8 11.6 %all-to-all-start.4 = ((f32[8,2,4096]{2,1,0:T(2,128)}), f32[8,2,4096]{2,1,0:T(2,128)S(1)}, u32[]{:S(2)}, u32[]{:S(2)}) async-start(f32[8,2,4096]{2,1,0:T(2,128)} %reshape.106), calls=%async_computation.4 | async-start | bytes 524288 | tf_op jit(solution)/shard_map/all_to_all | solution.py:81
  92.7 11.6 %all-to-all-start.5 = ((f32[8,2,4096]{2,1,0:T(2,128)}), f32[8,2,4096]{2,1,0:T(2,128)S(1)}, u32[]{:S(2)}, u32[]{:S(2)}) async-start(f32[8,2,4096]{2,1,0:T(2,128)} %reshape.108), calls=%async_computation.5 | async-start | bytes 524288 | tf_op jit(solution)/shard_map/all_to_all | solution.py:91
  96.1 79.4 %all-reduce.2.cloned.1.call-start = ((), (), s32[]{:S(2)}) async-start(), calls=%async_computation.7 | async-start | bytes 131072 | tf_op jit(solution)/shard_map/psum | solution.py:109
  105.7 1.2 copy-start.1
Sparse Core Ops, SparseCore 0:
  9.6 19.4 all-gather.1
  108.8 66.7 all-reduce.1
where the time goes:
time: 185 us; the launch traced here: 184 us
  waiting for transfers between devices  93.9 us (51%)
  starting transfers between devices  26.8 us (14%)
  local copies, waits for them, and re-layouts  22.8 us (12%)
  matrix products  22.1 us (12%)
  between operations  14.5 us (8%)
  other arithmetic  3.85 us (2%)
    psum x1, waiting for transfers between devices, on_device(): theta_grad = lax.psum(partial_grad, 'rows')  66.9 us
    all_to_all x2, waiting for transfers between devices, propagate(): lax.all_to_all(rpart.reshape(nrows, CAP, width * BLK), 'rows', split_axis...  11 us
    all_to_all x2, waiting for transfers between devices, propagate(): lax.all_to_all(outgoing, 'rows', split_axis=0, concat_axis=0, tiled=True)  9.33 us
    all_to_all x1, starting transfers between devices, on_device(): lax.all_to_all(remote_rxn, 'rows', split_axis=0, concat_axis=0, tiled=True)  7.41 us
    unnamed x26, local copies, waits for them, and re-layouts  7.4 us
    all_to_all x2, starting transfers between devices, propagate(): lax.all_to_all(outgoing, 'rows', split_axis=0, concat_axis=0, tiled=True)  7 us
    all_to_all x2, starting transfers between devices, propagate(): lax.all_to_all(rpart.reshape(nrows, CAP, width * BLK), 'rows', split_axis...  6.82 us
    all_to_all x1, starting transfers between devices, on_device(): lax.all_to_all(sent_count, 'rows', split_axis=0, concat_axis=0, tiled=True)  5.24 us
  transfers between devices with their start and end apart: 8, of which 7 were waited for; matrix products, arithmetic and copies ran while one was open for 10% of the time, Pallas kernels for 0%

commit v1 on v0

v1 whole, which is shorter than its diff:
```python
import functools

import jax
import jax.numpy as jnp
from jax import lax
from jax.experimental import pallas as pl
from jax.experimental.pallas import tpu as pltpu
from jax.sharding import PartitionSpec as P

BLK = 64
MB_DEV = 16
RB_DEV = 16
CAP = 2
MC = MB_DEV * BLK
RC = RB_DEV * BLK
SL = CAP * BLK
MESH = pl.DeviceIdType.MESH
F32 = jnp.float32
BF16 = jnp.bfloat16
NN = (((1,), (0,)), ((), ()))
NT = (((1,), (1,)), ((), ()))


def mm(a, b, dims):
    return lax.dot_general(a, b, dims, preferred_element_type=F32)


def split(v):
    hi = v.astype(BF16)
    lo = (v - hi.astype(F32)).astype(BF16)
    return hi, lo


def stack(v):
    return jnp.concatenate(split(v), axis=0)


def fold(p):
    half = p.shape[0] // 2
    return p[:half] + p[half:]


def local_kernel(mol_ref, rxn_ref, tiles_ref, h_ref):
    h_ref[...] = jnp.zeros_like(h_ref)
    half = lax.broadcasted_iota(jnp.int32, (BLK, 2 * BLK), 1) // BLK

    def place(k, carry):
        mol = mol_ref[k]
        rxn = rxn_ref[k]
        rows = pl.ds(pl.multiple_of(mol * BLK, BLK), BLK)
        cols = pl.ds(pl.multiple_of((rxn // 2) * 2 * BLK, 2 * BLK), 2 * BLK)
        tile = jnp.where(half == rxn % 2, tiles_ref[k].astype(F32), 0.0)
        h_ref[rows, cols] = (h_ref[rows, cols].astype(F32) + tile).astype(BF16)
        return carry

    lax.fori_loop(0, tiles_ref.shape[0], place, 0)


def main_kernel(
    n, nf, gs,
    x_ref, tht_ref, cot_ref, h_ref, t_ref, ids_ref,
    out_ref, grad_ref,
    gx, xh, xl, smat, emat, metas, metar, sbuf, rbuf, gsend, grecv, gsum, gfull,
    gx_s, gx_r, meta_s, meta_r, a2a_s, a2a_r, gr_s, gr_r, ga_s, ga_r,
):
    me = lax.axis_index("rows")
    fid = lax.axis_index("feat")
    groups = n // gs
    gw = gs * SL
    w = x_ref.shape[0]

    def each(count, body):
        if count == 1:
            body(0)
        else:
            def step(i, c):
                body(i)
                return c
            lax.fori_loop(0, count, step, 0)

    def peers(body):
        def step(k, c):
            body(lax.rem(me + k, n))
            return c
        lax.fori_loop(1, n, step, 0)

    barrier = pltpu.get_barrier_semaphore()
    peers(lambda d: pl.semaphore_signal(barrier, inc=1, device_id={"rows": d}, device_id_type=MESH))
    for k in range(1, nf):
        pl.semaphore_signal(
            barrier, inc=1, device_id={"feat": lax.rem(fid + k, nf)}, device_id_type=MESH
        )

    counts = jnp.sum(t_ref[...], axis=0, keepdims=True).astype(jnp.int32)
    first = lax.broadcasted_iota(jnp.int32, (8, SL), 0) == 0
    for d in range(n):
        cols = slice(d * SL, (d + 1) * SL)
        metas[d] = jnp.where(first, counts[:, cols], ids_ref[1:2, cols])
    pl.semaphore_wait(barrier, n - 1 + nf - 1)

    def feat_copy(src, dst, i, to):
        return pltpu.make_async_remote_copy(
            src_ref=src, dst_ref=dst, send_sem=gx_s.at[i], recv_sem=gx_r.at[i],
            device_id={"feat": to}, device_id_type=MESH,
        )

    relay = nf == 4
    hw = w // 2
    if relay:
        near = fid + 1 - 2 * lax.rem(fid, 2)
        far = lax.rem(fid + 2, 4)
        cross = lax.rem(near + 2, 4)
        rows2 = [pl.ds(0, hw), pl.ds(hw, hw)]
        c_far = [feat_copy(x_ref.at[r], gx.at[fid, r], 1 + i, far) for i, r in enumerate(rows2)]
        c_near = feat_copy(x_ref, gx.at[fid], 0, near)
        for c in c_far:
            c.start()
        c_near.start()
    else:
        direct = []
        for k in range(1, nf):
            direct.append(feat_copy(x_ref, gx.at[fid], k - 1, lax.rem(fid + k, nf)))
        for c in direct:
            c.start()

    def meta_copy(d, slot):
        return pltpu.make_async_remote_copy(
            src_ref=metas.at[d], dst_ref=metar.at[slot], send_sem=meta_s.at[d],
            recv_sem=meta_r.at[slot], device_id={"rows": d}, device_id_type=MESH,
        )

    peers(lambda d: meta_copy(d, me).start())
    metar[me] = metas[me]

    def fill_s(g):
        cols = pl.ds(pl.multiple_of(g * gw, SL), gw)
        tile = t_ref[:, cols]
        place = ids_ref[0:1, cols]
        for m in range(MB_DEV):
            smat[g, m * BLK:(m + 1) * BLK, :] = jnp.where(place == m, tile, 0.0).astype(BF16)

    each(groups, fill_s)

    ones = jnp.ones((16, MC), BF16)
    vdeg = 1.0 + mm(ones, h_ref[...], NT)
    if groups == 1:
        vdeg = vdeg + mm(jnp.ones((16, gw), BF16), smat[0], NT)
    else:
        vdeg = lax.fori_loop(
            0, groups, lambda g, v: v + mm(jnp.ones((16, gw), BF16), smat[g], NT), vdeg
        )
    vscale = (1.0 / jnp.sqrt(vdeg))[0:1]
    edeg = 1.0 + mm(ones, h_ref[...], NN)

    def split_in(f, v):
        hi, lo = split(v)
        at = pl.ds(pl.multiple_of(f * w, 16), w)
        xh[at, :] = hi
        xl[at, :] = lo

    split_in(fid, x_ref[...])

    if relay:
        c_fwd = []
        for i, r in enumerate(rows2):
            c_far[i].wait_recv()
            c = feat_copy(gx.at[far, r], gx.at[far, r], 3 + i, near)
            c.start()
            c_fwd.append(c)

    peers(lambda d: meta_copy(d, d).wait())
    state = [edeg]

    def fill_e(g, deg):
        for dd in range(gs):
            tgt = metar[g * gs + dd][1:2]
            rows = lax.broadcasted_iota(jnp.int32, (RC, SL), 0)
            emat[g, :, dd * SL:(dd + 1) * SL] = jnp.where(rows == tgt, 1.0, 0.0).astype(BF16)
        cnt = jnp.concatenate([metar[g * gs + dd] for dd in range(gs)], axis=1)
        cnt = jnp.broadcast_to(cnt[0:1], (16, gw)).astype(F32).astype(BF16)
        return deg + mm(cnt, emat[g], NT)

    if groups == 1:
        edeg = fill_e(0, edeg)
    else:
        edeg = lax.fori_loop(0, groups, fill_e, edeg)
    edeg = edeg[0:1]

    if relay:
        split_in(far, gx[far])
        c_near.wait_recv()
        split_in(near, gx[near])
        for c in c_fwd:
            c.wait_recv()
        split_in(cross, gx[cross])
        for c in [c_near] + c_far + c_fwd:
            c.wait_send()
    else:
        for k, c in enumerate(direct):
            c.wait()
            src = lax.rem(fid + nf - k - 1, nf)
            split_in(src, gx[src])

    th, tl = split(tht_ref[...])
    hidden = fold(mm(jnp.concatenate([th, tl], axis=0), xh[...], NN)) + mm(th, xl[...], NN)

    def a2a(phase, d, slot):
        return pltpu.make_async_remote_copy(
            src_ref=sbuf.at[phase, d], dst_ref=rbuf.at[phase, slot],
            send_sem=a2a_s.at[phase, d], recv_sem=a2a_r.at[phase, slot],
            device_id={"rows": d}, device_id_type=MESH,
        )

    def exchange(phase, lhs, mat):
        def part(g):
            p = fold(mm(lhs, mat[g], NN))
            for dd in range(gs):
                sbuf[phase, g * gs + dd] = p[:, dd * SL:(dd + 1) * SL]

        each(groups, part)
        peers(lambda d: a2a(phase, d, me).start())
        rbuf[phase, me] = sbuf[phase, me]

    def collect(phase, acc, mat):
        peers(lambda d: a2a(phase, d, d).wait())

        def add(g, a):
            got = jnp.concatenate([rbuf[phase, g * gs + dd] for dd in range(gs)], axis=1)
            return a + fold(mm(stack(got), mat[g], NT))

        if groups == 1:
            return add(0, acc)
        return lax.fori_loop(0, groups, add, acc)

    def propagate(values, phase):
        lhs = stack(values * vscale)
        exchange(phase, lhs, smat)
        acc = fold(mm(lhs, h_ref[...], NN))
        edge = collect(phase, acc, emat) / edeg
        lhs = stack(edge)
        exchange(phase + 1, lhs, emat)
        acc = fold(mm(lhs, h_ref[...], NT))
        return collect(phase + 1, acc, smat) * vscale

    output = jnp.tanh(propagate(hidden, 0))
    out_ref[...] = output
    gh, gl = split(propagate(cot_ref[...] * (1.0 - output * output), 2))
    partial = fold(mm(jnp.concatenate([gh, gl], axis=0), xh[...], NT)) + mm(gh, xl[...], NT)

    k = w // n
    for d in range(n):
        gsend[d] = partial[d * k:(d + 1) * k]

    def gr(d, slot):
        return pltpu.make_async_remote_copy(
            src_ref=gsend.at[d], dst_ref=grecv.at[slot], send_sem=gr_s.at[d],
            recv_sem=gr_r.at[slot], device_id={"rows": d}, device_id_type=MESH,
        )

    peers(lambda d: gr(d, me).start())
    grecv[me] = gsend[me]
    peers(lambda d: gr(d, d).wait())
    gsum[...] = jnp.sum(grecv[...], axis=0)

    def ga(d, slot):
        return pltpu.make_async_remote_copy(
            src_ref=gsum, dst_ref=gfull.at[slot], send_sem=ga_s.at[d],
            recv_sem=ga_r.at[slot], device_id={"rows": d}, device_id_type=MESH,
        )

    peers(lambda d: ga(d, me).start())
    gfull[me] = gsum[...]
    peers(lambda d: ga(d, d).wait())
    grad_ref[...] = gfull[...]


def on_device(
    node_feats, theta, cotangent, remote_mol, remote_rxn, remote_count, remote_tiles,
    local_mol, local_rxn, local_tiles,
):
    n = lax.axis_size("rows")
    nf = lax.axis_size("feat")
    gs = min(n, 8)
    groups = n // gs
    gw = gs * SL
    slots = n * CAP
    w, mols = node_feats.shape
    f = w * nf
    vmem = pl.BlockSpec(memory_space=pltpu.VMEM)
    smem = pl.BlockSpec(memory_space=pltpu.SMEM)

    ltiles = local_tiles.reshape(-1, BLK, BLK).astype(BF16)
    ltiles = jnp.concatenate([ltiles, ltiles], axis=2)
    dense = pl.pallas_call(
        local_kernel,
        out_shape=jax.ShapeDtypeStruct((MC, RC), BF16),
        in_specs=[smem, smem, vmem],
        out_specs=vmem,
        compiler_params=pltpu.CompilerParams(vmem_limit_bytes=16 * 2**20),
        name="local_incidence",
    )(local_mol, local_rxn, ltiles)

    live = (jnp.arange(CAP, dtype=jnp.int32)[None, :] < remote_count[:, None]).reshape(slots)
    rtiles = remote_tiles.reshape(slots, BLK, BLK).astype(F32)
    rtiles = jnp.where(live[:, None, None], rtiles, 0.0)
    rtiles = rtiles.transpose(1, 0, 2).reshape(BLK, slots * BLK)
    place = jnp.broadcast_to(remote_mol.reshape(slots, 1), (slots, BLK)).reshape(1, -1)
    target = (remote_rxn.reshape(slots, 1) * BLK + jnp.arange(BLK, dtype=jnp.int32)).reshape(1, -1)
    ids = jnp.concatenate([place, target], axis=0)

    dma = pltpu.SemaphoreType.DMA
    out, grad = pl.pallas_call(
        functools.partial(main_kernel, n, nf, gs),
        out_shape=(
            jax.ShapeDtypeStruct((w, mols), F32),
            jax.ShapeDtypeStruct((n, w // n, f), F32),
        ),
        in_specs=[vmem] * 6,
        out_specs=(vmem, vmem),
        scratch_shapes=[
            pltpu.VMEM((nf, w, mols), F32),
            pltpu.VMEM((f, mols), BF16),
            pltpu.VMEM((f, mols), BF16),
            pltpu.VMEM((groups, MC, gw), BF16),
            pltpu.VMEM((groups, RC, gw), BF16),
            pltpu.VMEM((n, 8, SL), jnp.int32),
            pltpu.VMEM((n, 8, SL), jnp.int32),
            pltpu.VMEM((4, n, w, SL), F32),
            pltpu.VMEM((4, n, w, SL), F32),
            pltpu.VMEM((n, w // n, f), F32),
            pltpu.VMEM((n, w // n, f), F32),
            pltpu.VMEM((w // n, f), F32),
            pltpu.VMEM((n, w // n, f), F32),
            dma((max(nf, 5),)), dma((max(nf, 5),)),
            dma((n,)), dma((n,)),
            dma((4, n)), dma((4, n)),
            dma((n,)), dma((n,)),
            dma((n,)), dma((n,)),
        ],
        compiler_params=pltpu.CompilerParams(
            collective_id=0, has_side_effects=True,
            vmem_limit_bytes=(28 + n // 2) * 2**20,
        ),
        name="train_step",
    )(node_feats, theta.T, cotangent, dense, rtiles, ids)
    return out, grad.reshape(w, f).T


def solution(mesh):
    return jax.shard_map(
        on_device,
        mesh=mesh,
        in_specs=(
            P("feat", "rows"),
            P(None, "feat"),
            P("feat", "rows"),
            P("rows", None),
            P("rows", None),
            P("rows"),
            P("rows", None, None),
            P("rows"),
            P("rows"),
            P("rows", None),
        ),
        out_specs=(P("feat", "rows"), P(None, "feat")),
        check_vma=False,
    )
```

time: 185 us -> 66.3 us (0.36)
  waiting for transfers between devices: 93.9 us -> 0 us
  Pallas kernels: 0 us -> 58.3 us
  starting transfers between devices: 26.8 us -> 0 us
  matrix products: 22.1 us -> 0 us
  local copies, waits for them, and re-layouts: 22.8 us -> 3.74 us
  between operations: 14.5 us -> 0.78 us
    psum x1 -> x0, waiting for transfers between devices: 66.9 us -> none  [on_device(): theta_grad = lax.psum(partial_grad, 'rows')]
    pallas_call x0 -> x2, Pallas kernels: none -> 58.3 us  [the longest x1 57 us: on_device(): pl.pallas_call(functools.partial(main_kernel, n, nf, gs), out_shape=(jax....]
    all_to_all x6 -> x0, starting transfers between devices: 26.5 us -> none  [the longest x1 7.41 us: on_device(): lax.all_to_all(remote_rxn, 'rows', split_axis=0, concat_axis=0, tiled=True)]
    all_to_all x6 -> x0, waiting for transfers between devices: 26.3 us -> none  [the longest x2 11 us: propagate(): lax.all_to_all(rpart.reshape(nrows, CAP, width * BLK), 'rows', split_axis...]
    dot_general x22 -> x0, matrix products: 22.1 us -> none  [the longest x2 3.74 us: propagate(): jnp.einsum('sij,scj->sci', ltiles, jnp.take(edge, local_rxn, axis=0), pre...]
    gather x8 -> x0, local copies, waits for them, and re-layouts: 6.46 us -> none  [the longest x2 2 us: propagate(): outgoing = jnp.take(edge, rxn_in, axis=0).reshape(nrows, CAP, width * BLK)]
    reshape x13 -> x2, local copies, waits for them, and re-layouts: 6.44 us -> 0.25 us  [the longest x1 0.17 us: on_device(): rtiles = rtiles.transpose(1, 0, 2).reshape(BLK, slots * BLK)]
    unnamed x26 -> x15, local copies, waits for them, and re-layouts: 7.4 us -> 2.12 us
  transfers between devices with their start and end apart: 8 -> 0, of which waited for: 7 -> 0; matrix products, arithmetic and copies ran while one was open for 10% -> 0% of each run, Pallas kernels for 0% -> 0%
where the time goes in v1:
time: 66.3 us; the launch traced here: 66.1 us
  Pallas kernels  58.3 us (88%)
  local copies, waits for them, and re-layouts  3.74 us (6%)
  other arithmetic  3.25 us (5%)
  between operations  0.78 us (1%)
    pallas_call x1, Pallas kernels, on_device(): pl.pallas_call(functools.partial(main_kernel, n, nf, gs), out_shape=(jax....  57 us
    unnamed x15, local copies, waits for them, and re-layouts  2.12 us

profile of v1, /device:TPU:0, one launch (start us, length us, event | category | flops | bytes accessed | tf_op | source)
XLA Modules:
  0.0 66.1 jit_solution(17549413378626674047)
XLA Ops:
  0.6 0.7 %broadcast_multiply_fusion = s32[8,2]{0,1:T(2,128)S(1)} fusion(s32[8,2]{0,1:T(2,128)} %param.14), kind=kLoop, calls=%fused_computation.6 | loop fusion | flops 16 | bytes 128 | tf_op jit(solution)/shard_map/mul | solution.py:308
  1.4 0.7 %iota_compare_fusion = pred[8,2]{1,0:T(8,128)(4,1)S(1)} fusion(s32[8]{0:T(128)} %param.15), kind=kLoop, calls=%fused_computation.5 | loop fusion | flops 16 | bytes 48 | tf_op jit(solution)/shard_map/lt | solution.py:303
  2.1 0.1 lt.23
  2.2 0.1 copy.17
  2.3 0.1 mul.12
  2.4 0.8 %copy.16 = s32[8,2]{1,0:T(8,128)S(1)} copy(s32[8,2]{0,1:T(2,128)} %param.13) | data formatting | bytes 128 | tf_op args[3]
  3.1 0.1 broadcast_in_dim.24
  3.2 0.1 broadcast_in_dim.25
  3.3 0.1 reshape.68
  3.4 0.1 iota_add_fusion
  3.4 0.1 add.26
  3.5 1.0 %convert_element_type.14 = f32[8,2,4096]{2,1,0:T(2,128)S(1)} convert(s32[8,2,4096]{2,1,0:T(2,128)} %param.16) | non-fusion elementwise | flops 65536 | bytes 524288 | tf_op jit(solution)/shard_map/convert_element_type | solution.py:304
  4.6 0.3 convert_element_type.15
  4.9 0.3 fusion
  5.3 0.2 reshape.67.t_ref
  5.5 0.0 copy-start
  5.5 0.0 copy-start.1
  5.5 0.0 copy-start.2
  5.5 0.5 convert_element_type.13
  6.1 0.3 pad_maximum_fusion.tiles_ref
  6.4 1.3 %local_incidence.1.h_ref = bf16[1024,1024]{1,0:T(8,128)(2,1)S(1)} custom-call(s32[32]{0:T(128)S(1)} %copy-done.3, s32[32]{0:T(128)S(1)} %copy-done.4, bf16[32,64,128]{2,1,0:T(8,128)(2,1)S(1)} %pad_maximum_fusion.tiles_ref), custom_call_target="tpu_custom_call" | custom-call | tf_op jit(solution)/shard_map/local_incidence/pallas_call | solution.py:294
  7.7 57.0 %train_step.1 = (f32[64,1024]{1,0:T(8,128)S(1)}, f32[8,8,256]{2,1,0:T(8,128)S(1)}) custom-call(f32[64,1024]{1,0:T(8,128)S(1)} %copy-done, f32[64,256]{1,0:T(8,128)S(1)} %bitcast.6, f32[64,1024]{1,0:T(8,128)S(1)} %copy-done.1, bf16[1024,1024]{1,0:T(8,128)(2,1)S(1)} %local_incidence.1.h_ref, f32[64,1024]{1,0:T(8,128)S(1)} %reshape.67.t_ref, ...), custom_call_target="tpu_custom_call" | custom-call | tf_op jit(solution)/shard_map/train_step/pallas_call | solution.py:312
  64.7 0.7 %copy.23 = f32[64,1024]{1,0:T(8,128)} copy(f32[64,1024]{1,0:T(8,128)S(1)} %get-tuple-element.8) | data formatting | bytes 524288
  65.5 0.6 copy.24
  (11 shorter events, 0.1 us)
Async XLA Ops:
  0.6 4.8 %copy-start.5 = (s32[32,4096]{1,0:T(8,128)S(1)}, s32[32,4096]{1,0:T(8,128)}, u32[]{:S(2)}) copy-start(s32[32,4096]{1,0:T(8,128)} %param.19) | copy-start | bytes 1572868
  4.9 1.5 %copy-start.3 = (s32[32]{0:T(128)S(1)}, s32[32]{0:T(128)}, u32[]{:S(2)}) copy-start(s32[32]{0:T(128)} %mol_ref.1) | copy-start | bytes 388
  4.9 1.5 %copy-start.4 = (s32[32]{0:T(128)S(1)}, s32[32]{0:T(128)}, u32[]{:S(2)}) copy-start(s32[32]{0:T(128)} %rxn_ref.1) | copy-start | bytes 388
  5.5 2.2 %copy-start = (f32[64,1024]{1,0:T(8,128)S(1)}, f32[64,1024]{1,0:T(8,128)}, u32[]{:S(2)}) copy-start(f32[64,1024]{1,0:T(8,128)} %x_ref.1) | copy-start | bytes 786436
  5.5 2.2 %copy-start.1 = (f32[64,1024]{1,0:T(8,128)S(1)}, f32[64,1024]{1,0:T(8,128)}, u32[]{:S(2)}) copy-start(f32[64,1024]{1,0:T(8,128)} %cot_ref.1) | copy-start | bytes 786436
  5.5 2.2 %copy-start.2 = (f32[256,64]{0,1:T(8,128)S(1)}, f32[256,64]{0,1:T(8,128)}, u32[]{:S(2)}) copy-start(f32[256,64]{0,1:T(8,128)} %param.11) | copy-start | bytes 196612

commit v2 on v1

--- a/solution.py
+++ b/solution.py
@@ -11,6 +11,7 @@
 MB_DEV = 16
 RB_DEV = 16
 CAP = 2
+PARTS = 2
 MC = MB_DEV * BLK
 RC = RB_DEV * BLK
 SL = CAP * BLK
@@ -96,41 +97,12 @@
     for d in range(n):
         cols = slice(d * SL, (d + 1) * SL)
         metas[d] = jnp.where(first, counts[:, cols], ids_ref[1:2, cols])
-    pl.semaphore_wait(barrier, n - 1 + nf - 1)
-
-    def feat_copy(src, dst, i, to):
-        return pltpu.make_async_remote_copy(
-            src_ref=src, dst_ref=dst, send_sem=gx_s.at[i], recv_sem=gx_r.at[i],
-            device_id={"feat": to}, device_id_type=MESH,
-        )
-
-    relay = nf == 4
-    hw = w // 2
-    if relay:
-        near = fid + 1 - 2 * lax.rem(fid, 2)
-        far = lax.rem(fid + 2, 4)
-        cross = lax.rem(near + 2, 4)
-        rows2 = [pl.ds(0, hw), pl.ds(hw, hw)]
-        c_far = [feat_copy(x_ref.at[r], gx.at[fid, r], 1 + i, far) for i, r in enumerate(rows2)]
-        c_near = feat_copy(x_ref, gx.at[fid], 0, near)
-        for c in c_far:
-            c.start()
-        c_near.start()
-    else:
-        direct = []
-        for k in range(1, nf):
-            direct.append(feat_copy(x_ref, gx.at[fid], k - 1, lax.rem(fid + k, nf)))
-        for c in direct:
-            c.start()
 
     def meta_copy(d, slot):
         return pltpu.make_async_remote_copy(
             src_ref=metas.at[d], dst_ref=metar.at[slot], send_sem=meta_s.at[d],
             recv_sem=meta_r.at[slot], device_id={"rows": d}, device_id_type=MESH,
         )
-
-    peers(lambda d: meta_copy(d, me).start())
-    metar[me] = metas[me]
 
     def fill_s(g):
         cols = pl.ds(pl.multiple_of(g * gw, SL), gw)
@@ -150,26 +122,53 @@
             0, groups, lambda g, v: v + mm(jnp.ones((16, gw), BF16), smat[g], NT), vdeg
         )
     vscale = (1.0 / jnp.sqrt(vdeg))[0:1]
+
+    hw = w // PARTS
+    parts = [slice(i * hw, (i + 1) * hw) for i in range(PARTS)]
+
+    def a2a(phase, i, d, slot):
+        return pltpu.make_async_remote_copy(
+            src_ref=sbuf.at[phase, i, d], dst_ref=rbuf.at[phase, i, slot],
+            send_sem=a2a_s.at[phase, i, d], recv_sem=a2a_r.at[phase, i, slot],
+            device_id={"rows": d}, device_id_type=MESH,
+        )
+
+    def produce(phase, i, lhs, mat):
+        def part(g):
+            p = fold(mm(lhs, mat[g], NN))
+            for dd in range(gs):
+                sbuf[phase, i, g * gs + dd] = p[:, dd * SL:(dd + 1) * SL]
+
+        each(groups, part)
+
+    def send(phase, i):
+        peers(lambda d: a2a(phase, i, d, me).start())
+        rbuf[phase, i, me] = sbuf[phase, i, me]
+
+    def collect(phase, i, acc, mat):
+        peers(lambda d: a2a(phase, i, d, d).wait())
+
+        def add(g, a):
+            got = jnp.concatenate([rbuf[phase, i, g * gs + dd] for dd in range(gs)], axis=1)
+            return a + fold(mm(stack(got), mat[g], NT))
+
+        if groups == 1:
+            return add(0, acc)
+        return lax.fori_loop(0, groups, add, acc)
+
+    lhs = [stack(x_ref[p, :] * vscale) for p in parts]
+    produce(0, 0, lhs[0], smat)
+    pl.semaphore_wait(barrier, n - 1 + nf - 1)
+    peers(lambda d: meta_copy(d, me).start())
+    metar[me] = metas[me]
+    send(0, 0)
+    for i in range(1, PARTS):
+        produce(0, i, lhs[i], smat)
+        send(0, i)
+
     edeg = 1.0 + mm(ones, h_ref[...], NN)
-
-    def split_in(f, v):
-        hi, lo = split(v)
-        at = pl.ds(pl.multiple_of(f * w, 16), w)
-        xh[at, :] = hi
-        xl[at, :] = lo
-
-    split_in(fid, x_ref[...])
-
-    if relay:
-        c_fwd = []
-        for i, r in enumerate(rows2):
-            c_far[i].wait_recv()
-            c = feat_copy(gx.at[far, r], gx.at[far, r], 3 + i, near)
-            c.start()
-            c_fwd.append(c)
-
+    acc = [fold(mm(v, h_ref[...], NN)) for v in lhs]
     peers(lambda d: meta_copy(d, d).wait())
-    state = [edeg]
 
     def fill_e(g, deg):
         for dd in range(gs):
@@ -186,65 +185,68 @@
         edeg = lax.fori_loop(0, groups, fill_e, edeg)
     edeg = edeg[0:1]
 
+    lhs = []
+    for i in range(PARTS):
+        lhs.append(stack(collect(0, i, acc[i], emat) / edeg))
+        produce(1, i, lhs[i], emat)
+        send(1, i)
+    acc = [fold(mm(v, h_ref[...], NT)) for v in lhs]
+
+    def feat_copy(slot, p, i, to):
+        ref = gx.at[slot, pl.ds(p * hw, hw)]
+        return pltpu.make_async_remote_copy(
+            src_ref=ref, dst_ref=ref, send_sem=gx_s.at[i, p], recv_sem=gx_r.at[i, p],
+            device_id={"feat": to}, device_id_type=MESH,
+        )
+
+    def split_in(f, p):
+        hi, lo = split(gx[f, p * hw:(p + 1) * hw, :])
+        at = pl.ds(pl.multiple_of(f * w + p * hw, 16), hw)
+        xh[at, :] = hi
+        xl[at, :] = lo
+
+    relay = nf == 4
+    near = fid + 1 - 2 * lax.rem(fid, 2)
+    far = lax.rem(fid + 2, nf)
+    cross = lax.rem(near + 2, nf)
+    sent = []
+    for i in range(PARTS):
+        gx[fid, parts[i], :] = collect(1, i, acc[i], smat) * vscale
+        if relay:
+            c = [feat_copy(fid, i, 0, far), feat_copy(fid, i, 1, near)]
+        else:
+            c = [feat_copy(fid, i, k - 1, lax.rem(fid + k, nf)) for k in range(1, nf)]
+        for one in c:
+            one.start()
+        sent.append(c)
+    for i in range(PARTS):
+        split_in(fid, i)
     if relay:
-        split_in(far, gx[far])
-        c_near.wait_recv()
-        split_in(near, gx[near])
-        for c in c_fwd:
-            c.wait_recv()
-        split_in(cross, gx[cross])
-        for c in [c_near] + c_far + c_fwd:
+        passed = []
+        for i in range(PARTS):
+            sent[i][0].wait_recv()
+            c = feat_copy(far, i, 2, near)
+            c.start()
+            passed.append(c)
+            split_in(far, i)
+            sent[i][1].wait_recv()
+            split_in(near, i)
+        for i in range(PARTS):
+            passed[i].wait_recv()
+            split_in(cross, i)
+        for c in passed + sum(sent, []):
             c.wait_send()
     else:
-        for k, c in enumerate(direct):
-            c.wait()
-            src = lax.rem(fid + nf - k - 1, nf)
-            split_in(src, gx[src])
+        for i in range(PARTS):
+            for k, c in enumerate(sent[i]):
+                c.wait()
+                split_in(lax.rem(fid + nf - k - 1, nf), i)
 
     th, tl = split(tht_ref[...])
-    hidden = fold(mm(jnp.concatenate([th, tl], axis=0), xh[...], NN)) + mm(th, xl[...], NN)
-
-    def a2a(phase, d, slot):
-        return pltpu.make_async_remote_copy(
-            src_ref=sbuf.at[phase, d], dst_ref=rbuf.at[phase, slot],
-            send_sem=a2a_s.at[phase, d], recv_sem=a2a_r.at[phase, slot],
-            device_id={"rows": d}, device_id_type=MESH,
-        )
-
-    def exchange(phase, lhs, mat):
-        def part(g):
-            p = fold(mm(lhs, mat[g], NN))
-            for dd in range(gs):
-                sbuf[phase, g * gs + dd] = p[:, dd * SL:(dd + 1) * SL]
-
-        each(groups, part)
-        peers(lambda d: a2a(phase, d, me).start())
-        rbuf[phase, me] = sbuf[phase, me]
-
-    def collect(phase, acc, mat):
-        peers(lambda d: a2a(phase, d, d).wait())
-
-        def add(g, a):
-            got = jnp.concatenate([rbuf[phase, g * gs + dd] for dd in range(gs)], axis=1)
-            return a + fold(mm(stack(got), mat[g], NT))
-
-        if groups == 1:
-            return add(0, acc)
-        return lax.fori_loop(0, groups, add, acc)
-
-    def propagate(values, phase):
-        lhs = stack(values * vscale)
-        exchange(phase, lhs, smat)
-        acc = fold(mm(lhs, h_ref[...], NN))
-        edge = collect(phase, acc, emat) / edeg
-        lhs = stack(edge)
-        exchange(phase + 1, lhs, emat)
-        acc = fold(mm(lhs, h_ref[...], NT))
-        return collect(phase + 1, acc, smat) * vscale
-
-    output = jnp.tanh(propagate(hidden, 0))
+    mixed = fold(mm(jnp.concatenate([th, tl], axis=0), xh[...], NN)) + mm(th, xl[...], NN)
+    output = jnp.tanh(mixed)
     out_ref[...] = output
-    gh, gl = split(propagate(cot_ref[...] * (1.0 - output * output), 2))
+    gh, gl = split(cot_ref[...] * (1.0 - output * output))
     partial = fold(mm(jnp.concatenate([gh, gl], axis=0), xh[...], NT)) + mm(gh, xl[...], NT)
 
     k = w // n
@@ -325,15 +327,15 @@
             pltpu.VMEM((groups, RC, gw), BF16),
             pltpu.VMEM((n, 8, SL), jnp.int32),
             pltpu.VMEM((n, 8, SL), jnp.int32),
-            pltpu.VMEM((4, n, w, SL), F32),
-            pltpu.VMEM((4, n, w, SL), F32),
+            pltpu.VMEM((2, PARTS, n, w // PARTS, SL), F32),
+            pltpu.VMEM((2, PARTS, n, w // PARTS, SL), F32),
             pltpu.VMEM((n, w // n, f), F32),
             pltpu.VMEM((n, w // n, f), F32),
             pltpu.VMEM((w // n, f), F32),
             pltpu.VMEM((n, w // n, f), F32),
-            dma((max(nf, 5),)), dma((max(nf, 5),)),
+            dma((max(nf - 1, 3), PARTS)), dma((max(nf - 1, 3), PARTS)),
             dma((n,)), dma((n,)),
-            dma((4, n)), dma((4, n)),
+            dma((2, PARTS, n)), dma((2, PARTS, n)),
             dma((n,)), dma((n,)),
             dma((n,)), dma((n,)),
         ],

time: 66.3 us -> 46.9 us (0.71)
  Pallas kernels: 58.3 us -> 39 us
    pallas_call x1, Pallas kernels: 57 us -> 37.6 us  [on_device(): pl.pallas_call(functools.partial(main_kernel, n, nf, gs), out_shape=(jax....]
where the time goes in v2:
time: 46.9 us; the launch traced here: 46.7 us
  Pallas kernels  39 us (83%)
  local copies, waits for them, and re-layouts  3.74 us (8%)
  other arithmetic  3.25 us (7%)
  between operations  0.78 us (2%)
    pallas_call x1, Pallas kernels, on_device(): pl.pallas_call(functools.partial(main_kernel, n, nf, gs), out_shape=(jax....  37.6 us
    unnamed x15, local copies, waits for them, and re-layouts  2.12 us
    pallas_call x1, Pallas kernels, on_device(): pl.pallas_call(local_kernel, out_shape=jax.ShapeDtypeStruct((MC, RC), BF1...  1.32 us
    convert_element_type x1, other arithmetic, on_device(): rtiles = remote_tiles.reshape(slots, BLK, BLK).astype(F32)  1.04 us

profile of v2, /device:TPU:0, one launch (start us, length us, event | category | flops | bytes accessed | tf_op | source)
XLA Modules:
  0.0 46.7 jit_solution(17283690037885973039)
XLA Ops:
  0.6 0.7 %broadcast_multiply_fusion = s32[8,2]{0,1:T(2,128)S(1)} fusion(s32[8,2]{0,1:T(2,128)} %param.14), kind=kLoop, calls=%fused_computation.6 | loop fusion | flops 16 | bytes 128 | tf_op jit(solution)/shard_map/mul | solution.py:310
  1.4 0.7 %iota_compare_fusion = pred[8,2]{1,0:T(8,128)(4,1)S(1)} fusion(s32[8]{0:T(128)} %param.15), kind=kLoop, calls=%fused_computation.5 | loop fusion | flops 16 | bytes 48 | tf_op jit(solution)/shard_map/lt | solution.py:305
  2.1 0.1 lt.23
  2.2 0.1 copy.17
  2.3 0.1 mul.12
  2.4 0.8 %copy.16 = s32[8,2]{1,0:T(8,128)S(1)} copy(s32[8,2]{0,1:T(2,128)} %param.13) | data formatting | bytes 128 | tf_op args[3]
  3.1 0.1 broadcast_in_dim.24
  3.2 0.1 broadcast_in_dim.25
  3.3 0.1 reshape.68
  3.4 0.1 iota_add_fusion
  3.4 0.1 add.26
  3.5 1.0 %convert_element_type.14 = f32[8,2,4096]{2,1,0:T(2,128)S(1)} convert(s32[8,2,4096]{2,1,0:T(2,128)} %param.16) | non-fusion elementwise | flops 65536 | bytes 524288 | tf_op jit(solution)/shard_map/convert_element_type | solution.py:306
  4.6 0.3 convert_element_type.15
  4.9 0.3 fusion
  5.3 0.2 reshape.67.t_ref
  5.5 0.0 copy-start
  5.5 0.0 copy-start.1
  5.5 0.0 copy-start.2
  5.5 0.5 %convert_element_type.13 = bf16[32,64,64]{2,1,0:T(8,128)(2,1)S(1)} reshape(bf16[32,4096]{1,0:T(8,128)(2,1)S(1)} %convert_element_type.12) | data formatting | bytes 524288 | tf_op jit(solution)/shard_map/convert_element_type | solution.py:294
  6.1 0.3 pad_maximum_fusion.tiles_ref
  6.4 1.3 %local_incidence.1.h_ref = bf16[1024,1024]{1,0:T(8,128)(2,1)S(1)} custom-call(s32[32]{0:T(128)S(1)} %copy-done.3, s32[32]{0:T(128)S(1)} %copy-done.4, bf16[32,64,128]{2,1,0:T(8,128)(2,1)S(1)} %pad_maximum_fusion.tiles_ref), custom_call_target="tpu_custom_call" | custom-call | tf_op jit(solution)/shard_map/local_incidence/pallas_call | solution.py:296
  7.7 37.6 %train_step.1 = (f32[64,1024]{1,0:T(8,128)S(1)}, f32[8,8,256]{2,1,0:T(8,128)S(1)}) custom-call(f32[64,1024]{1,0:T(8,128)S(1)} %copy-done, f32[64,256]{1,0:T(8,128)S(1)} %bitcast.6, f32[64,1024]{1,0:T(8,128)S(1)} %copy-done.1, bf16[1024,1024]{1,0:T(8,128)(2,1)S(1)} %local_incidence.1.h_ref, f32[64,1024]{1,0:T(8,128)S(1)} %reshape.67.t_ref, ...), custom_call_target="tpu_custom_call" | custom-call | tf_op jit(solution)/shard_map/train_step/pallas_call | solution.py:314
  45.4 0.7 %copy.23 = f32[64,1024]{1,0:T(8,128)} copy(f32[64,1024]{1,0:T(8,128)S(1)} %get-tuple-element.8) | data formatting | bytes 524288
  46.1 0.6 %copy.24 = f32[256,64]{0,1:T(8,128)} copy(f32[256,64]{0,1:T(8,128)S(1)} %bitcast.7) | data formatting | bytes 131072
  (11 shorter events, 0.1 us)
Async XLA Ops:
  0.6 4.8 %copy-start.5 = (s32[32,4096]{1,0:T(8,128)S(1)}, s32[32,4096]{1,0:T(8,128)}, u32[]{:S(2)}) copy-start(s32[32,4096]{1,0:T(8,128)} %param.19) | copy-start | bytes 1572868
  4.9 1.5 %copy-start.3 = (s32[32]{0:T(128)S(1)}, s32[32]{0:T(128)}, u32[]{:S(2)}) copy-start(s32[32]{0:T(128)} %mol_ref.1) | copy-start | bytes 388
  4.9 1.5 %copy-start.4 = (s32[32]{0:T(128)S(1)}, s32[32]{0:T(128)}, u32[]{:S(2)}) copy-start(s32[32]{0:T(128)} %rxn_ref.1) | copy-start | bytes 388
  5.5 2.2 %copy-start = (f32[64,1024]{1,0:T(8,128)S(1)}, f32[64,1024]{1,0:T(8,128)}, u32[]{:S(2)}) copy-start(f32[64,1024]{1,0:T(8,128)} %x_ref.1) | copy-start | bytes 786436
  5.5 2.2 %copy-start.1 = (f32[64,1024]{1,0:T(8,128)S(1)}, f32[64,1024]{1,0:T(8,128)}, u32[]{:S(2)}) copy-start(f32[64,1024]{1,0:T(8,128)} %cot_ref.1) | copy-start | bytes 786436
  5.5 2.2 %copy-start.2 = (f32[256,64]{0,1:T(8,128)S(1)}, f32[256,64]{0,1:T(8,128)}, u32[]{:S(2)}) copy-start(f32[256,64]{0,1:T(8,128)} %param.11) | copy-start | bytes 196612

commit v3 on v2

--- a/solution.py
+++ b/solution.py
@@ -54,12 +54,12 @@
         h_ref[rows, cols] = (h_ref[rows, cols].astype(F32) + tile).astype(BF16)
         return carry
 
-    lax.fori_loop(0, tiles_ref.shape[0], place, 0)
+    lax.fori_loop(0, tiles_ref.shape[0], place, 0, unroll=4)
 
 
 def main_kernel(
     n, nf, gs,
-    x_ref, tht_ref, cot_ref, h_ref, t_ref, ids_ref,
+    x_ref, tht_ref, cot_ref, h_ref, t_ref, mol_ref, rxn_ref, cnt_ref,
     out_ref, grad_ref,
     gx, xh, xl, smat, emat, metas, metar, sbuf, rbuf, gsend, grecv, gsum, gfull,
     gx_s, gx_r, meta_s, meta_r, a2a_s, a2a_r, gr_s, gr_r, ga_s, ga_r,
@@ -92,26 +92,26 @@
             barrier, inc=1, device_id={"feat": lax.rem(fid + k, nf)}, device_id_type=MESH
         )
 
-    counts = jnp.sum(t_ref[...], axis=0, keepdims=True).astype(jnp.int32)
     first = lax.broadcasted_iota(jnp.int32, (8, SL), 0) == 0
+    lane = lax.broadcasted_iota(jnp.int32, (1, SL), 1)
+    slot = lane // BLK
     for d in range(n):
-        cols = slice(d * SL, (d + 1) * SL)
-        metas[d] = jnp.where(first, counts[:, cols], ids_ref[1:2, cols])
+        live = slot < cnt_ref[d]
+        place = jnp.where(live, jnp.where(slot == 0, mol_ref[0, d], mol_ref[1, d]), -1)
+        target = jnp.where(slot == 0, rxn_ref[0, d], rxn_ref[1, d]) * BLK + lane % BLK
+        tile = jnp.where(live, t_ref[:, d * SL:(d + 1) * SL], 0.0)
+        counts = jnp.sum(tile, axis=0, keepdims=True).astype(jnp.int32)
+        metas[d] = jnp.where(first, counts, target)
+        at = slice((d % gs) * SL, (d % gs + 1) * SL)
+        for m in range(MB_DEV):
+            here = jnp.where(place == m, tile, 0.0)
+            smat[d // gs, m * BLK:(m + 1) * BLK, at] = here.astype(BF16)
 
     def meta_copy(d, slot):
         return pltpu.make_async_remote_copy(
             src_ref=metas.at[d], dst_ref=metar.at[slot], send_sem=meta_s.at[d],
             recv_sem=meta_r.at[slot], device_id={"rows": d}, device_id_type=MESH,
         )
-
-    def fill_s(g):
-        cols = pl.ds(pl.multiple_of(g * gw, SL), gw)
-        tile = t_ref[:, cols]
-        place = ids_ref[0:1, cols]
-        for m in range(MB_DEV):
-            smat[g, m * BLK:(m + 1) * BLK, :] = jnp.where(place == m, tile, 0.0).astype(BF16)
-
-    each(groups, fill_s)
 
     ones = jnp.ones((16, MC), BF16)
     vdeg = 1.0 + mm(ones, h_ref[...], NT)
@@ -157,17 +157,16 @@
         return lax.fori_loop(0, groups, add, acc)
 
     lhs = [stack(x_ref[p, :] * vscale) for p in parts]
-    produce(0, 0, lhs[0], smat)
+    for i in range(PARTS):
+        produce(0, i, lhs[i], smat)
+    edeg = 1.0 + mm(ones, h_ref[...], NN)
+    acc = [fold(mm(v, h_ref[...], NN)) for v in lhs]
     pl.semaphore_wait(barrier, n - 1 + nf - 1)
     peers(lambda d: meta_copy(d, me).start())
     metar[me] = metas[me]
-    send(0, 0)
-    for i in range(1, PARTS):
-        produce(0, i, lhs[i], smat)
+    for i in range(PARTS):
         send(0, i)
 
-    edeg = 1.0 + mm(ones, h_ref[...], NN)
-    acc = [fold(mm(v, h_ref[...], NN)) for v in lhs]
     peers(lambda d: meta_copy(d, d).wait())
 
     def fill_e(g, deg):
@@ -302,13 +301,8 @@
         name="local_incidence",
     )(local_mol, local_rxn, ltiles)
 
-    live = (jnp.arange(CAP, dtype=jnp.int32)[None, :] < remote_count[:, None]).reshape(slots)
     rtiles = remote_tiles.reshape(slots, BLK, BLK).astype(F32)
-    rtiles = jnp.where(live[:, None, None], rtiles, 0.0)
     rtiles = rtiles.transpose(1, 0, 2).reshape(BLK, slots * BLK)
-    place = jnp.broadcast_to(remote_mol.reshape(slots, 1), (slots, BLK)).reshape(1, -1)
-    target = (remote_rxn.reshape(slots, 1) * BLK + jnp.arange(BLK, dtype=jnp.int32)).reshape(1, -1)
-    ids = jnp.concatenate([place, target], axis=0)
 
     dma = pltpu.SemaphoreType.DMA
     out, grad = pl.pallas_call(
@@ -317,7 +311,7 @@
             jax.ShapeDtypeStruct((w, mols), F32),
             jax.ShapeDtypeStruct((n, w // n, f), F32),
         ),
-        in_specs=[vmem] * 6,
+        in_specs=[vmem] * 5 + [smem] * 3,
         out_specs=(vmem, vmem),
         scratch_shapes=[
             pltpu.VMEM((nf, w, mols), F32),
@@ -344,7 +338,7 @@
             vmem_limit_bytes=(28 + n // 2) * 2**20,
         ),
         name="train_step",
-    )(node_feats, theta.T, cotangent, dense, rtiles, ids)
+    )(node_feats, theta.T, cotangent, dense, rtiles, remote_mol.T, remote_rxn.T, remote_count)
     return out, grad.reshape(w, f).T
 
 

time: 46.9 us -> 44 us (0.938)
  other arithmetic: 3.25 us -> 1.42 us
  local copies, waits for them, and re-layouts: 3.74 us -> 2.74 us
    unnamed x15 -> x20, local copies, waits for them, and re-layouts: 2.12 us -> 1.38 us
    mul x1 -> x0, other arithmetic: 0.74 us -> none  [on_device(): remote_rxn.reshape(slots, 1) * BLK + jnp.arange(BLK, dtype=jnp.int32)]
    lt x1 -> x0, other arithmetic: 0.73 us -> none  [on_device(): jnp.arange(CAP, dtype=jnp.int32)[None, :] < remote_count[:, None]]
where the time goes in v3:
time: 44 us; the launch traced here: 43.9 us
  Pallas kernels  38.9 us (88%)
  local copies, waits for them, and re-layouts  2.74 us (6%)
  other arithmetic  1.42 us (3%)
  between operations  0.81 us (2%)
    pallas_call x1, Pallas kernels, on_device(): pl.pallas_call(functools.partial(main_kernel, n, nf, gs), out_shape=(jax....  37.9 us
    unnamed x20, local copies, waits for them, and re-layouts  1.38 us
    convert_element_type x1, other arithmetic, on_device(): rtiles = remote_tiles.reshape(slots, BLK, BLK).astype(F32)  1.1 us
    pallas_call x1, Pallas kernels, on_device(): pl.pallas_call(local_kernel, out_shape=jax.ShapeDtypeStruct((MC, RC), BF1...  1.07 us

profile of v3, /device:TPU:0, one launch (start us, length us, event | category | flops | bytes accessed | tf_op | source)
XLA Modules:
  0.0 43.9 jit_solution(5880552133240458273)
XLA Ops:
  0.6 0.0 copy-start.8
  0.6 1.1 %convert_element_type.14 = f32[8,2,4096]{2,1,0:T(2,128)S(1)} convert(s32[8,2,4096]{2,1,0:T(2,128)} %param.16) | non-fusion elementwise | flops 65536 | bytes 524288 | tf_op jit(solution)/shard_map/convert_element_type | solution.py:304
  1.7 0.3 convert_element_type.15
  2.1 0.3 copy.14
  2.4 0.2 reshape.14.t_ref
  2.6 0.0 copy-done.8
  2.6 0.0 copy-start
  2.6 0.0 copy-start.1
  2.7 0.0 copy-start.2
  2.7 0.0 copy-start.3
  2.7 0.0 copy-start.4
  2.7 0.0 copy-start.7
  2.7 0.5 %convert_element_type.13 = bf16[32,64,64]{2,1,0:T(8,128)(2,1)S(1)} reshape(bf16[32,4096]{1,0:T(8,128)(2,1)S(1)} %convert_element_type.12) | data formatting | bytes 524288 | tf_op jit(solution)/shard_map/convert_element_type | solution.py:293
  3.2 0.3 pad_maximum_fusion.tiles_ref
  3.5 0.0 copy-done.5
  3.6 0.0 copy-done.6
  3.6 1.1 %local_incidence.1.h_ref = bf16[1024,1024]{1,0:T(8,128)(2,1)S(1)} custom-call(s32[32]{0:T(128)S(1)} %copy-done.5, s32[32]{0:T(128)S(1)} %copy-done.6, bf16[32,64,128]{2,1,0:T(8,128)(2,1)S(1)} %pad_maximum_fusion.tiles_ref), custom_call_target="tpu_custom_call" | custom-call | tf_op jit(solution)/shard_map/local_incidence/pallas_call | solution.py:295
  4.6 0.0 copy-done
  4.7 0.0 copy-done.1
  4.7 0.0 copy-done.2
  4.7 0.0 copy-done.3
  4.7 37.9 %train_step.1 = (f32[64,1024]{1,0:T(8,128)S(1)}, f32[8,8,256]{2,1,0:T(8,128)S(1)}) custom-call(f32[64,1024]{1,0:T(8,128)S(1)} %copy-done, f32[64,256]{1,0:T(8,128)S(1)} %bitcast.9, f32[64,1024]{1,0:T(8,128)S(1)} %copy-done.1, bf16[1024,1024]{1,0:T(8,128)(2,1)S(1)} %local_incidence.1.h_ref, f32[64,1024]{1,0:T(8,128)S(1)} %reshape.14.t_ref, ...), custom_call_target="tpu_custom_call" | custom-call | tf_op jit(solution)/shard_map/train_step/pallas_call | solution.py:308
  42.6 0.7 %copy.17 = f32[64,1024]{1,0:T(8,128)} copy(f32[64,1024]{1,0:T(8,128)S(1)} %get-tuple-element.8) | data formatting | bytes 524288
  43.3 0.6 %copy.18 = f32[256,64]{0,1:T(8,128)} copy(f32[256,64]{0,1:T(8,128)S(1)} %bitcast.10) | data formatting | bytes 131072
  (5 shorter events, 0.0 us)
Async XLA Ops:
  0.6 2.0 %copy-start.8 = (s32[32,4096]{1,0:T(8,128)S(1)}, s32[32,4096]{1,0:T(8,128)}, u32[]{:S(2)}) copy-start(s32[32,4096]{1,0:T(8,128)} %param.19) | copy-start | bytes 1572868
  2.1 1.5 %copy-start.5 = (s32[32]{0:T(128)S(1)}, s32[32]{0:T(128)}, u32[]{:S(2)}) copy-start(s32[32]{0:T(128)} %mol_ref.1) | copy-start | bytes 388
  2.1 1.5 %copy-start.6 = (s32[32]{0:T(128)S(1)}, s32[32]{0:T(128)}, u32[]{:S(2)}) copy-start(s32[32]{0:T(128)} %rxn_ref.1) | copy-start | bytes 388
  2.6 2.0 %copy-start = (f32[64,1024]{1,0:T(8,128)S(1)}, f32[64,1024]{1,0:T(8,128)}, u32[]{:S(2)}) copy-start(f32[64,1024]{1,0:T(8,128)} %x_ref.1) | copy-start | bytes 786436
  2.6 2.0 %copy-start.1 = (f32[64,1024]{1,0:T(8,128)S(1)}, f32[64,1024]{1,0:T(8,128)}, u32[]{:S(2)}) copy-start(f32[64,1024]{1,0:T(8,128)} %cot_ref.1) | copy-start | bytes 786436
  2.7 2.0 %copy-start.2 = (f32[256,64]{0,1:T(8,128)S(1)}, f32[256,64]{0,1:T(8,128)}, u32[]{:S(2)}) copy-start(f32[256,64]{0,1:T(8,128)} %param.11) | copy-start | bytes 196612
  2.7 2.0 %copy-start.3 = (s32[8,2]{0,1:T(2,128)S(1)}, s32[8,2]{0,1:T(2,128)}, u32[]{:S(2)}) copy-start(s32[8,2]{0,1:T(2,128)} %param.13) | copy-start | bytes 196
  2.7 2.0 %copy-start.4 = (s32[8,2]{0,1:T(2,128)S(1)}, s32[8,2]{0,1:T(2,128)}, u32[]{:S(2)}) copy-start(s32[8,2]{0,1:T(2,128)} %param.14) | copy-start | bytes 196
  2.7 2.0 %copy-start.7 = (s32[8]{0:T(128)S(1)}, s32[8]{0:T(128)}, u32[]{:S(2)}) copy-start(s32[8]{0:T(128)} %cnt_ref.1) | copy-start | bytes 100

commit v4 on v3

--- a/solution.py
+++ b/solution.py
@@ -99,7 +99,7 @@
         live = slot < cnt_ref[d]
         place = jnp.where(live, jnp.where(slot == 0, mol_ref[0, d], mol_ref[1, d]), -1)
         target = jnp.where(slot == 0, rxn_ref[0, d], rxn_ref[1, d]) * BLK + lane % BLK
-        tile = jnp.where(live, t_ref[:, d * SL:(d + 1) * SL], 0.0)
+        tile = jnp.where(live, t_ref[:, d * SL:(d + 1) * SL].astype(F32), 0.0)
         counts = jnp.sum(tile, axis=0, keepdims=True).astype(jnp.int32)
         metas[d] = jnp.where(first, counts, target)
         at = slice((d % gs) * SL, (d % gs + 1) * SL)
@@ -146,7 +146,7 @@
         rbuf[phase, i, me] = sbuf[phase, i, me]
 
     def collect(phase, i, acc, mat):
-        peers(lambda d: a2a(phase, i, d, d).wait())
+        peers(lambda d: a2a(phase, i, d, d).wait_recv())
 
         def add(g, a):
             got = jnp.concatenate([rbuf[phase, i, g * gs + dd] for dd in range(gs)], axis=1)
@@ -167,7 +167,7 @@
     for i in range(PARTS):
         send(0, i)
 
-    peers(lambda d: meta_copy(d, d).wait())
+    peers(lambda d: meta_copy(d, d).wait_recv())
 
     def fill_e(g, deg):
         for dd in range(gs):
@@ -233,12 +233,12 @@
         for i in range(PARTS):
             passed[i].wait_recv()
             split_in(cross, i)
-        for c in passed + sum(sent, []):
-            c.wait_send()
+        unsent = passed + sum(sent, [])
     else:
+        unsent = sum(sent, [])
         for i in range(PARTS):
             for k, c in enumerate(sent[i]):
-                c.wait()
+                c.wait_recv()
                 split_in(lax.rem(fid + nf - k - 1, nf), i)
 
     th, tl = split(tht_ref[...])
@@ -260,7 +260,7 @@
 
     peers(lambda d: gr(d, me).start())
     grecv[me] = gsend[me]
-    peers(lambda d: gr(d, d).wait())
+    peers(lambda d: gr(d, d).wait_recv())
     gsum[...] = jnp.sum(grecv[...], axis=0)
 
     def ga(d, slot):
@@ -271,6 +271,13 @@
 
     peers(lambda d: ga(d, me).start())
     gfull[me] = gsum[...]
+    for c in unsent:
+        c.wait_send()
+    peers(lambda d: meta_copy(d, d).wait_send())
+    peers(lambda d: gr(d, d).wait_send())
+    for phase in range(2):
+        for i in range(PARTS):
+            peers(lambda d: a2a(phase, i, d, d).wait_send())
     peers(lambda d: ga(d, d).wait())
     grad_ref[...] = gfull[...]
 
@@ -301,7 +308,7 @@
         name="local_incidence",
     )(local_mol, local_rxn, ltiles)
 
-    rtiles = remote_tiles.reshape(slots, BLK, BLK).astype(F32)
+    rtiles = remote_tiles.reshape(slots, BLK, BLK).astype(BF16)
     rtiles = rtiles.transpose(1, 0, 2).reshape(BLK, slots * BLK)
 
     dma = pltpu.SemaphoreType.DMA

time: 44 us -> 43.1 us (0.980)
  Pallas kernels: 38.9 us -> 38.2 us
    convert_element_type x1, other arithmetic: 0.03 us -> 1.08 us  [on_device(): ltiles = local_tiles.reshape(-1, BLK, BLK).astype(BF16)]
    convert_element_type x1, other arithmetic: 1.1 us -> 0.09 us  [on_device(): rtiles = remote_tiles.reshape(slots, BLK, BLK).astype(BF16)]
    pallas_call x1, Pallas kernels: 37.9 us -> 37.1 us  [on_device(): pl.pallas_call(functools.partial(main_kernel, n, nf, gs), out_shape=(jax....]
where the time goes in v4:
time: 43.1 us; the launch traced here: 43 us
  Pallas kernels  38.2 us (89%)
  local copies, waits for them, and re-layouts  2.51 us (6%)
  other arithmetic  1.47 us (3%)
  between operations  0.83 us (2%)
    pallas_call x1, Pallas kernels, on_device(): pl.pallas_call(functools.partial(main_kernel, n, nf, gs), out_shape=(jax....  37.1 us
    unnamed x20, local copies, waits for them, and re-layouts  1.39 us
    convert_element_type x1, other arithmetic, on_device(): ltiles = local_tiles.reshape(-1, BLK, BLK).astype(BF16)  1.08 us
    pallas_call x1, Pallas kernels, on_device(): pl.pallas_call(local_kernel, out_shape=jax.ShapeDtypeStruct((MC, RC), BF1...  1.07 us

profile of v4, /device:TPU:0, one launch (start us, length us, event | category | flops | bytes accessed | tf_op | source)
XLA Modules:
  0.0 43.0 jit_solution(4605839952863706793)
XLA Ops:
  0.6 0.0 copy-start.5
  0.6 0.0 copy-start.6
  0.7 1.1 %convert_element_type.12 = bf16[32,4096]{1,0:T(8,128)(2,1)S(1)} convert(s32[32,4096]{1,0:T(8,128)} %param.19) | non-fusion elementwise | flops 131072 | bytes 786432 | tf_op jit(solution)/shard_map/convert_element_type | solution.py:300
  1.7 0.0 copy-start.8
  1.7 0.5 %convert_element_type.13 = bf16[32,64,64]{2,1,0:T(8,128)(2,1)S(1)} reshape(bf16[32,4096]{1,0:T(8,128)(2,1)S(1)} %convert_element_type.12) | data formatting | bytes 524288 | tf_op jit(solution)/shard_map/convert_element_type | solution.py:300
  2.3 0.3 pad_maximum_fusion.tiles_ref
  2.6 0.0 copy-done.5
  2.6 0.0 copy-done.6
  2.6 0.0 copy-start
  2.6 0.0 copy-start.1
  2.6 0.0 copy-start.2
  2.6 0.0 copy-start.3
  2.7 0.0 copy-start.4
  2.7 0.0 copy-start.7
  2.7 1.1 %local_incidence.1.h_ref = bf16[1024,1024]{1,0:T(8,128)(2,1)S(1)} custom-call(s32[32]{0:T(128)S(1)} %copy-done.5, s32[32]{0:T(128)S(1)} %copy-done.6, bf16[32,64,128]{2,1,0:T(8,128)(2,1)S(1)} %pad_maximum_fusion.tiles_ref), custom_call_target="tpu_custom_call" | custom-call | tf_op jit(solution)/shard_map/local_incidence/pallas_call | solution.py:302
  3.8 0.0 copy-done.8
  3.8 0.1 convert_element_type.14
  3.9 0.2 convert_element_type.15
  4.1 0.2 copy.14
  4.3 0.2 reshape.14.t_ref
  4.5 0.0 copy-done
  4.5 37.1 %train_step.1 = (f32[64,1024]{1,0:T(8,128)S(1)}, f32[8,8,256]{2,1,0:T(8,128)S(1)}) custom-call(f32[64,1024]{1,0:T(8,128)S(1)} %copy-done, f32[64,256]{1,0:T(8,128)S(1)} %bitcast.9, f32[64,1024]{1,0:T(8,128)S(1)} %copy-done.1, bf16[1024,1024]{1,0:T(8,128)(2,1)S(1)} %local_incidence.1.h_ref, bf16[64,1024]{1,0:T(8,128)(2,1)S(1)} %reshape.14.t_ref, ...), custom_call_target="tpu_custom_call" | custom-call | tf_op jit(solution)/shard_map/train_step/pallas_call | solution.py:315
  41.7 0.7 %copy.17 = f32[64,1024]{1,0:T(8,128)} copy(f32[64,1024]{1,0:T(8,128)S(1)} %get-tuple-element.8) | data formatting | bytes 524288
  42.4 0.6 %copy.18 = f32[256,64]{0,1:T(8,128)} copy(f32[256,64]{0,1:T(8,128)S(1)} %bitcast.10) | data formatting | bytes 131072
  (5 shorter events, 0.0 us)
Async XLA Ops:
  0.6 2.0 %copy-start.5 = (s32[32]{0:T(128)S(1)}, s32[32]{0:T(128)}, u32[]{:S(2)}) copy-start(s32[32]{0:T(128)} %mol_ref.1) | copy-start | bytes 388
  0.6 2.0 %copy-start.6 = (s32[32]{0:T(128)S(1)}, s32[32]{0:T(128)}, u32[]{:S(2)}) copy-start(s32[32]{0:T(128)} %rxn_ref.1) | copy-start | bytes 388
  1.7 2.0 %copy-start.8 = (s32[8,2,4096]{2,1,0:T(2,128)S(1)}, s32[8,2,4096]{2,1,0:T(2,128)}, u32[]{:S(2)}) copy-start(s32[8,2,4096]{2,1,0:T(2,128)} %param.16) | copy-start | bytes 786436
  2.6 1.9 %copy-start = (f32[64,1024]{1,0:T(8,128)S(1)}, f32[64,1024]{1,0:T(8,128)}, u32[]{:S(2)}) copy-start(f32[64,1024]{1,0:T(8,128)} %x_ref.1) | copy-start | bytes 786436
  2.6 1.9 %copy-start.1 = (f32[64,1024]{1,0:T(8,128)S(1)}, f32[64,1024]{1,0:T(8,128)}, u32[]{:S(2)}) copy-start(f32[64,1024]{1,0:T(8,128)} %cot_ref.1) | copy-start | bytes 786436
  2.6 1.9 %copy-start.2 = (f32[256,64]{0,1:T(8,128)S(1)}, f32[256,64]{0,1:T(8,128)}, u32[]{:S(2)}) copy-start(f32[256,64]{0,1:T(8,128)} %param.11) | copy-start | bytes 196612
  2.6 1.9 %copy-start.3 = (s32[8,2]{0,1:T(2,128)S(1)}, s32[8,2]{0,1:T(2,128)}, u32[]{:S(2)}) copy-start(s32[8,2]{0,1:T(2,128)} %param.13) | copy-start | bytes 196
  2.7 1.9 %copy-start.4 = (s32[8,2]{0,1:T(2,128)S(1)}, s32[8,2]{0,1:T(2,128)}, u32[]{:S(2)}) copy-start(s32[8,2]{0,1:T(2,128)} %param.14) | copy-start | bytes 196
  2.7 1.9 %copy-start.7 = (s32[8]{0:T(128)S(1)}, s32[8]{0:T(128)}, u32[]{:S(2)}) copy-start(s32[8]{0:T(128)} %cnt_ref.1) | copy-start | bytes 100
